TPU v7x, 32 devices: a whole 2x2x4 slice. The times are simulated.
32 devices in a mesh: areal: 16 (over z, y, x), layer: 2 (over core).
Axes of the slice: x: 2, y: 2, z: 4, core: 2. Of those that a mesh axis runs over, the one named last changes fastest.
Arguments:
- rhs: bfloat16 [16, 4, 112, 384], P('areal', 'layer'), may hold values from -6 to 6
- areal_blocks: bfloat16 [16, 4, 6, 384, 384], P('areal', 'layer'), may hold values from -0.078125 to 0.078125
- vertical_blocks: bfloat16 [16, 4, 2, 384, 384], P('areal', 'layer'), may hold values from -0.078125 to 0.078125
- conn_src: int32 [16, 2, 6], P('areal', 'layer'), may hold values from 0 to 31, as said below
- conn_count: int32 [16, 2], P('areal', 'layer'), may hold values from 1 to 6, as said below
- tile_map: int32 [32], replicated, may hold values from 0 to 31, as said below
- well_cells: int32 [16, 4, 4], P('areal', 'layer'), may hold values from 0 to 127
- well_gain: float32 [16, 4, 4], P('areal', 'layer'), may hold values from -24 to 24
- sens: float32 [16, 4, 3, 128], P('areal', 'layer'), may hold values from -6 to 6
- basis: bfloat16 [16, 4, 128, 256], P('areal', 'layer'), may hold values from -0.0625 to 0.0625
Outputs:
- adjoint: bfloat16 [16, 4, 112, 384], P('areal', 'layer')
- coefficients: bfloat16 [112, 256], P('layer', 'areal')
Inputs may be any that keep to these rules, and one draw needn't show every extreme that they name: Tile t of a layer group's plane is held by device column tile_map[t] // 2 in tile layer 2 g + tile_map[t] % 2; each value is held by one tile. `conn_src`: the 6 sources of device column c lie, in some order, on the 6 device columns (c + k) mod 16 with k one of 1 to 2, their negatives, 8 and 9, one on each. `conn_count`: the live connections of a device are its first ones. `well_cells`: cells of a tile, repeats allowed.
All inputs are finite; a program needn't handle non-finite values.
Results may differ from a plain program's by a relative error of at most 0.02.
Values may be sent and summed in bfloat16 or wider, within the bound.
No kernel may reach another device: no remote copies, remote signals or barrier semaphores. Data moves between devices by JAX's collectives and lax.ppermute only.
A program may use at most 64 MiB of HBM per device.

v0:
```python
import jax
import jax.numpy as jnp
from jax import lax
from jax.sharding import PartitionSpec as P

ITERS = 3


def extended(x, sides, width):
    for axis, dim in sides:
        size, length = (lax.axis_size(axis), x.shape[dim])
        up = [(i, (i + 1) % size) for i in range(size - 1)]
        down = [(j, i) for i, j in up]
        last = lax.slice_in_dim(x, length - width, length, axis=dim)
        leading = lax.slice_in_dim(x, 0, width, axis=dim)
        before = lax.ppermute(last, axis, up)
        after = lax.ppermute(leading, axis, down)
        x = jnp.concatenate([before, x, after], axis=dim)
    return x


def on_device(
    rhs,
    areal_blocks,
    vertical_blocks,
    conn_src,
    conn_count,
    tile_map,
    well_cells,
    well_gain,
    sens,
    basis,
):
    cells = sens.shape[-1]
    phases = sens.shape[-2]
    rows = rhs.shape[2]
    sources = conn_src[0, 0]
    place = jnp.take(tile_map, sources)
    peer = place // 2
    slot = place % 2
    live = jnp.arange(sources.shape[0], dtype=jnp.int32) < conn_count[0, 0]
    blocks = areal_blocks[0]
    vert_blocks = vertical_blocks[0]
    rhs_float = rhs[0].astype(jnp.float32)
    lam = rhs
    for step in range(ITERS):
        whole = lax.all_gather(lam, "areal", axis=0, tiled=True)
        chosen = whole[peer, slot]
        chosen = jnp.where(live[:, None, None], chosen, jnp.zeros_like(chosen))
        padded = extended(lam, (("layer", 1),), 1)[0]
        near = jnp.stack([padded[0:2], padded[2:4]], axis=1)
        off = jnp.einsum("sru,dsuv->drv", chosen, blocks, preferred_element_type=jnp.float32)
        off = off + jnp.einsum(
            "dkru,dkuv->drv", near, vert_blocks, preferred_element_type=jnp.float32
        )
        lam = (rhs_float - off).astype(jnp.bfloat16)[None]
    lamf = lam[0].astype(jnp.float32).reshape(2, rows, phases, cells)
    grad = jnp.sum(lamf * sens[0][:, None, :, :], axis=2)
    hits = well_cells[0][:, :, None] == jnp.arange(cells, dtype=jnp.int32)[None, None, :]
    well_sum = jnp.sum(jnp.where(hits, well_gain[0][:, :, None], 0.0), axis=1)
    grad = (grad + well_sum[:, None, :] * lamf[:, :, 0, :]).astype(jnp.bfloat16)
    partial_sum = jnp.einsum("jrc,jcm->rm", grad, basis[0], preferred_element_type=jnp.float32)
    reduced = lax.psum_scatter(partial_sum, "areal", scatter_dimension=1, tiled=True)
    reduced = lax.psum_scatter(reduced, "layer", scatter_dimension=0, tiled=True)
    return (lam, reduced.astype(jnp.bfloat16))


def solution(mesh):
    in_specs = (
        P("areal", "layer", None, None),
        P("areal", "layer", None, None, None),
        P("areal", "layer", None, None, None),
        P("areal", "layer", None),
        P("areal", "layer"),
        P(),
        P("areal", "layer", None),
        P("areal", "layer", None),
        P("areal", "layer", None, None),
        P("areal", "layer", None, None),
    )
    out_specs = (P("areal", "layer", None, None), P("layer", "areal"))
    return jax.shard_map(
        on_device, mesh=mesh, in_specs=in_specs, out_specs=out_specs, check_vma=False
    )
```

profile of v0, /device:TPU:0, one launch (start us, length us, event | category | flops | bytes accessed | tf_op | source)
XLA Modules:
  0.0 313.6 jit_solution(6981233226110270401)
XLA Ops:
  8.0 1.9 fusion.93
  9.8 3.0 collective-permute-start
  15.4 1.3 gather_fusion
  18.5 2.4 convolution_bitcast_fusion.2
  20.9 57.5 %all-gather.6.cloned.1.call-done = bf16[16,2,112,384]{3,2,1,0:T(8,128)(2,1)} async-done(((bf16[1,2,112,384]{3,2,1,0:T(8,128)(2,1)}), bf16[16,2,112,384]{3,2,1,0:T(8,128)(2,1)}) %all-gather.6.cloned.1.call-update) | async-done | bytes 2752528 | tf_op jit(solution)/shard_map/all_gather | solution.py:47
  78.3 3.2 %gather_fusion.1 = bf16[6,112,384]{2,1,0:T(8,128)(2,1)} fusion(bf16[16,2,112,384]{3,2,1,0:T(8,128)(2,1)} %all-gather.6.cloned.1.call-done, s32[6]{0:T(128)S(1)} %fusion.82), kind=kCustom, calls=%fused_computation.1 | custom fusion | bytes 1032240 | tf_op jit(solution)/shard_map/gather | solution.py:48
  81.6 2.5 fusion.33
  85.1 1.3 collective-permute-start.2
  86.4 1.3 collective-permute-start.3
  87.8 1.9 collective-permute-done.3
  90.6 2.4 convolution_bitcast_fusion.1
  93.0 55.1 %all-gather.8.cloned.1.call-done = bf16[32,112,384]{2,1,0:T(8,128)(2,1)} async-done(((bf16[2,112,384]{2,1,0:T(8,128)(2,1)}), bf16[32,112,384]{2,1,0:T(8,128)(2,1)}) %all-gather.8.cloned.1.call-update) | async-done | bytes 2752528 | tf_op jit(solution)/shard_map/all_gather | solution.py:47
  148.1 3.2 %gather_fusion.2 = bf16[6,112,384]{2,1,0:T(8,128)(2,1)} fusion(bf16[16,2,112,384]{3,2,1,0:T(8,128)(2,1)} %bitcast.156, s32[6]{0:T(128)S(1)} %fusion.82), kind=kCustom, calls=%fused_computation.2 | custom fusion | bytes 1032240 | tf_op jit(solution)/shard_map/gather | solution.py:48
  151.4 2.5 fusion.36
  155.0 1.3 collective-permute-start.4
  156.3 1.3 collective-permute-start.5
  160.4 2.4 convolution_bitcast_fusion
  162.8 55.1 %all-gather.10.cloned.1.call-done = bf16[32,112,384]{2,1,0:T(8,128)(2,1)} async-done(((bf16[2,112,384]{2,1,0:T(8,128)(2,1)}), bf16[32,112,384]{2,1,0:T(8,128)(2,1)}) %all-gather.10.cloned.1.call-update) | async-done | bytes 2752528 | tf_op jit(solution)/shard_map/all_gather | solution.py:47
  217.9 3.2 %gather_fusion.3 = bf16[6,112,384]{2,1,0:T(8,128)(2,1)} fusion(bf16[16,2,112,384]{3,2,1,0:T(8,128)(2,1)} %bitcast.155, s32[6]{0:T(128)S(1)} %fusion.82), kind=kCustom, calls=%fused_computation.3 | custom fusion | bytes 1032240 | tf_op jit(solution)/shard_map/gather | solution.py:48
  221.2 2.6 fusion.39
  223.7 1.8 copy.31
  226.7 1.9 convolution_bitcast_fusion.3
  229.9 73.9 %reduce-scatter.3.cloned.1.call-done = f32[112,16]{0,1:T(8,128)} async-done(((f32[112,256]{0,1:T(8,128)}), f32[112,16]{0,1:T(8,128)}) %reduce-scatter.3.cloned.1.call-update) | async-done | bytes 7184 | tf_op jit(solution)/shard_map/reduce_scatter | solution.py:63
  303.8 2.6 all-reduce
  (34 shorter events, 12.8 us)
Async XLA Ops:
  7.2 74.4 %copy-start = (bf16[1,2,6,384,384]{4,3,2,1,0:T(8,128)(2,1)S(1)}, bf16[1,2,6,384,384]{4,3,2,1,0:T(8,128)(2,1)}, u32[]{:S(2)}) copy-start(bf16[1,2,6,384,384]{4,3,2,1,0:T(8,128)(2,1)} %param.11) | copy-start | bytes 10616836
  7.2 71.2 %all-gather.6.cloned.1.call-start = ((), (), s32[]{:S(2)}) async-start(), calls=%async_computation.1 | async-start | bytes 2924544 | tf_op jit(solution)/shard_map/all_gather | solution.py:47
  7.9 140.2 %all-gather.8.cloned.1.call-start = ((), (), s32[]{:S(2)}) async-start(), calls=%async_computation.3 | async-start | bytes 2924544 | tf_op jit(solution)/shard_map/all_gather | solution.py:47
  9.8 7.6 %collective-permute-start = (bf16[1,1,112,384]{3,2,1,0:T(8,128)(2,1)}, bf16[1,1,112,384]{3,2,1,0:T(8,128)(2,1)}, u32[]{:S(2)}, u32[]{:S(2)}) collective-permute-start(bf16[1,1,112,384]{3,2,1,0:T(8,128)(2,1)} %get-tuple-element.12), channel_id=1, source_target_pairs={{0,1},{2,3},{4,5},{6,7},{8,9},{10,11},{12,13},{14,15},{16,17},{18,... | collective-permute-start | bytes 258056 | tf_op jit(solution)/shard_map/ppermute | solution.py:16
  12.8 4.6 %collective-permute-start.1 = (bf16[1,1,112,384]{3,2,1,0:T(8,128)(2,1)}, bf16[1,1,112,384]{3,2,1,0:T(8,128)(2,1)}, u32[]{:S(2)}, u32[]{:S(2)}) collective-permute-start(bf16[1,1,112,384]{3,2,1,0:T(8,128)(2,1)} %get-tuple-element.13), channel_id=1, source_target_pairs={{1,0},{3,2},{5,4},{7,6},{9,8},{11,10},{13,12},{15,14},{17,16},{19,... | collective-permute-start | bytes 258056 | tf_op jit(solution)/shard_map/ppermute | solution.py:17
  84.1 133.8 %all-gather.10.cloned.1.call-start = ((), (), s32[]{:S(2)}) async-start(), calls=%async_computation.4 | async-start | bytes 2924544 | tf_op jit(solution)/shard_map/all_gather | solution.py:47
  85.1 2.6 collective-permute-start.2
  86.4 3.2 %collective-permute-start.3 = (bf16[1,1,112,384]{3,2,1,0:T(8,128)(2,1)S(1)}, bf16[1,1,112,384]{3,2,1,0:T(8,128)(2,1)S(1)}, u32[]{:S(2)}, u32[]{:S(2)}) collective-permute-start(bf16[1,1,112,384]{3,2,1,0:T(8,128)(2,1)S(1)} %get-tuple-element.9), channel_id=1, source_target_pairs={{1,0},{3,2},{5,4},{7,6},{9,8},{11,10},{13,12},{15,14},{17,16},{19,... | collective-permute-start | bytes 258056 | tf_op jit(solution)/shard_map/ppermute | solution.py:17
  148.1 5.9 %copy-start.1 = (f32[1,2,3,128]{3,1,2,0:T(2,128)S(1)}, f32[1,2,3,128]{3,1,2,0:T(2,128)}, u32[]{:S(2)}) copy-start(f32[1,2,3,128]{3,1,2,0:T(2,128)} %param.18) | copy-start | bytes 9220
  153.9 149.9 %reduce-scatter.3.cloned.1.call-start = ((), (), s32[]{:S(2)}) async-start(), calls=%async_computation.2 | async-start | bytes 139264 | tf_op jit(solution)/shard_map/reduce_scatter | solution.py:63
  155.0 3.4 %collective-permute-start.4 = (bf16[1,1,112,384]{3,2,1,0:T(8,128)(2,1)S(1)}, bf16[1,1,112,384]{3,2,1,0:T(8,128)(2,1)S(1)}, u32[]{:S(2)}, u32[]{:S(2)}) collective-permute-start(bf16[1,1,112,384]{3,2,1,0:T(8,128)(2,1)S(1)} %get-tuple-element.4), channel_id=1, source_target_pairs={{0,1},{2,3},{4,5},{6,7},{8,9},{10,11},{12,13},{14,15},{16,17},{18,... | collective-permute-start | bytes 258056 | tf_op jit(solution)/shard_map/ppermute | solution.py:16
  156.3 3.2 %collective-permute-start.5 = (bf16[1,1,112,384]{3,2,1,0:T(8,128)(2,1)S(1)}, bf16[1,1,112,384]{3,2,1,0:T(8,128)(2,1)S(1)}, u32[]{:S(2)}, u32[]{:S(2)}) collective-permute-start(bf16[1,1,112,384]{3,2,1,0:T(8,128)(2,1)S(1)} %get-tuple-element.5), channel_id=1, source_target_pairs={{1,0},{3,2},{5,4},{7,6},{9,8},{11,10},{13,12},{15,14},{17,16},{19,... | collective-permute-start | bytes 258056 | tf_op jit(solution)/shard_map/ppermute | solution.py:17
  221.2 7.5 %copy-start.2 = (u32[32]{0:T(128)S(1)}, u32[32]{0:T(128)}, u32[]{:S(2)}) copy-start(u32[32]{0:T(128)} %constant.99) | copy-start | bytes 388
Sparse Core Ops, SparseCore 0:
  10.8 67.4 all-gather.5
  84.3 63.8 all-gather.7
  154.1 63.8 all-gather.9
  228.7 75.0 reduce-scatter.2
where the time goes:
time: 314 us
  waiting for transfers between devices  245 us (78%)
  local copies, waits for them, and re-layouts  17.8 us (6%)
  matrix products  16.7 us (5%)
  between operations  15.2 us (5%)
  starting transfers between devices  9.6 us (3%)
  other arithmetic  6.32 us (2%)
    all_gather x3, waiting for transfers between devices, on_device(): whole = lax.all_gather(lam, 'areal', axis=0, tiled=True)  168 us
    reduce_scatter x1, waiting for transfers between devices, on_device(): lax.psum_scatter(partial_sum, 'areal', scatter_dimension=1, tiled=True)  73.9 us
    gather x3, local copies, waits for them, and re-layouts, on_device(): chosen = whole[peer, slot]  9.65 us
    dot_general x3, matrix products, on_device(): jnp.einsum('sru,dsuv->drv', chosen, blocks, preferred_element_type=jnp.fl...  7.65 us
    dot_general x3, matrix products, on_device(): jnp.einsum('dkru,dkuv->drv', near, vert_blocks, preferred_element_type=jn...  7.17 us
  transfers between devices with their start and end apart: 10, of which 6 were waited for; matrix products, arithmetic and copies ran while one was open for 6% of the time, Pallas kernels for 0%

commit v1 on v0

v1 whole, which is shorter than its diff:
```python
import functools

import jax
import jax.numpy as jnp
from jax import lax
from jax.experimental import pallas as pl
from jax.experimental.pallas import tpu as pltpu
from jax.sharding import PartitionSpec as P

ITERS = 3
F32 = jnp.float32
BF16 = jnp.bfloat16
SMEM = pl.BlockSpec(memory_space=pltpu.SMEM)
VMEM = pl.BlockSpec(memory_space=pltpu.VMEM)
LIMIT = 32 * 1024 * 1024


def near_steps(count):
    near = list(range(1, count // 2))
    return near + [-k for k in near]


def far_steps(columns):
    return [columns // 2, columns // 2 + 1]


def held(x):
    return pltpu.with_memory_space_constraint(x, pltpu.VMEM)


def dot(a, b):
    return jnp.dot(a, b, preferred_element_type=F32)


def plan_kernel(columns, steps, src, count, tile_map, me, meta, *asks):
    number = len(steps)
    conn = [0] * number
    slots = [0] * number
    for s in range(number):
        place = tile_map[src[s]]
        peer = lax.shift_right_logical(place, 1)
        slot = lax.bitwise_and(place, 1)
        away = peer - me[0]
        away = jnp.where(away < 0, away + columns, away)
        for i, k in enumerate(steps):
            hit = away == k % columns
            conn[i] = jnp.where(hit, s, conn[i])
            slots[i] = jnp.where(hit, slot, slots[i])
    for i in range(number):
        meta[i] = conn[i]
        meta[number + i] = slots[i]
        meta[2 * number + i] = jnp.where(conn[i] < count[0], 1, 0)
        asks[i][...] = jnp.full(asks[i].shape, slots[i], jnp.int32).astype(F32)


def pick_kernel(number, rhs, *refs):
    wanted, sends = refs[:number], refs[number:]
    low, high = rhs[0].astype(F32), rhs[1].astype(F32)
    for mask, send in zip(wanted, sends):
        send[...] = jnp.where(mask[0:1, :] > 0.5, high, low).astype(BF16)


def own_kernel(lam, rhs, vert, part):
    part[0] = rhs[0].astype(F32) - dot(lam[1], vert[0, 1])
    part[1] = rhs[1].astype(F32) - dot(lam[0], vert[1, 0])


def gather_rows(number, pairs, meta, arrived, joined):
    width = arrived[0].shape[-1]
    for i in range(number):
        tile = arrived[i][meta[number + i]] if pairs[i] else arrived[i][...]
        tile = jnp.where(meta[2 * number + i] > 0, tile, jnp.zeros_like(tile))
        at = pl.multiple_of(meta[i] * width, 128)
        joined[:, pl.ds(at, width)] = tile


def updated(number, pairs, two, paired, meta, group, part, blocks, vert, arrived, beside, joined, total):
    gather_rows(number, pairs, meta, arrived, joined)
    rows = joined[...]
    depth, width = rows.shape[1], blocks.shape[-1]
    for d in range(2):
        total[d] = part[d] - dot(rows, blocks[d].reshape(depth, width))
    if two:
        mine = group[0]
        d = 1 - mine
        other = beside[0][mine] if paired else beside[0][...]
        total[d] = total[d] - dot(other, vert[d, d])
    else:
        for d in range(2):
            other = beside[d][1 - d] if paired else beside[d][...]
            total[d] = total[d] - dot(other, vert[d, d])


def apply_kernel(number, pairs, two, paired, meta, group, part, blocks, vert, *refs):
    sides = 1 if two else 2
    arrived, refs = refs[:number], refs[number:]
    beside, refs = refs[:sides], refs[sides:]
    wanted, refs = refs[:number], refs[number:]
    lam, sends, refs = refs[0], refs[1 : 1 + number], refs[1 + number :]
    outer, (joined, total) = refs[:sides], refs[sides:]
    updated(number, pairs, two, paired, meta, group, part, blocks, vert, arrived, beside, joined, total)
    low, high = total[0], total[1]
    lam[0] = low.astype(BF16)
    lam[1] = high.astype(BF16)
    for mask, send in zip(wanted, sends):
        send[...] = jnp.where(mask[0:1, :] > 0.5, high, low).astype(BF16)
    if two:
        outer[0][...] = jnp.where(group[0] == 0, high, low).astype(BF16)
    else:
        outer[0][...] = high.astype(BF16)
        outer[1][...] = low.astype(BF16)


def last_kernel(number, pairs, two, paired, columns, groups, meta, group, wells, gains, part, blocks, vert, sens, basis, *refs):
    sides = 1 if two else 2
    arrived, refs = refs[:number], refs[number:]
    beside, refs = refs[:sides], refs[sides:]
    lam, pieces, joined, total = refs
    updated(number, pairs, two, paired, meta, group, part, blocks, vert, arrived, beside, joined, total)
    cells = sens.shape[-1]
    phases = sens.shape[-2]
    spot = lax.broadcasted_iota(jnp.int32, (1, cells), 1)
    projected = None
    for d in range(2):
        rounded = total[d].astype(BF16)
        lam[d] = rounded
        back = rounded.astype(F32)
        well = jnp.zeros((1, cells), F32)
        for w in range(wells.shape[1]):
            well = well + jnp.where(spot == wells[d, w], gains[d, w], 0.0)
        grad = back[:, :cells] * (sens[d, 0:1, :] + well)
        for p in range(1, phases):
            grad = grad + back[:, p * cells : (p + 1) * cells] * sens[d, p : p + 1, :]
        term = dot(grad.astype(BF16), basis[d])
        projected = term if projected is None else projected + term
    if two:
        turned = projected.T
        modes, rows = turned.shape
        share, half = modes // columns, rows // 2
        for c in range(columns):
            top = turned[c * share : c * share + share // 2]
            low = turned[c * share + share // 2 : (c + 1) * share]
            for g in range(2):
                cut = slice(g * half, (g + 1) * half)
                pieces[2 * c + g] = jnp.concatenate([top[:, cut], low[:, cut]], axis=1)
    else:
        pieces[...] = projected


def sum_kernel(pieces, out):
    total = pieces[0]
    for i in range(1, pieces.shape[0]):
        total = total + pieces[i]
    half = total.shape[1] // 2
    joined = jnp.concatenate([total[:, :half], total[:, half:]], axis=0)
    out[...] = joined.T.astype(BF16)


def call(kernel, outs, ins, specs, scratch=(), flops=0, out_specs=None):
    return pl.pallas_call(
        kernel,
        out_shape=outs,
        in_specs=specs,
        out_specs=out_specs or [VMEM] * len(outs),
        scratch_shapes=list(scratch),
        compiler_params=pltpu.CompilerParams(vmem_limit_bytes=LIMIT),
        cost_estimate=pl.CostEstimate(flops=flops, bytes_accessed=flops // 200, transcendentals=0),
    )(*ins)


def shift(x, k):
    columns = lax.axis_size("areal")
    return held(lax.ppermute(x, "areal", [(i, (i - k) % columns) for i in range(columns)]))


def beside_layers(tiles, whole):
    groups = lax.axis_size("layer")
    if groups == 2:
        return [held(lax.ppermute(tiles[0], "layer", [(0, 1), (1, 0)]))]
    up = [(i, i + 1) for i in range(groups - 1)]
    down = [(i + 1, i) for i in range(groups - 1)]
    first, second = (tiles[0], tiles[0]) if whole else tiles
    return [held(lax.ppermute(first, "layer", up)), held(lax.ppermute(second, "layer", down))]


def on_device(
    rhs,
    areal_blocks,
    vertical_blocks,
    conn_src,
    conn_count,
    tile_map,
    well_cells,
    well_gain,
    sens,
    basis,
):
    columns = lax.axis_size("areal")
    groups = lax.axis_size("layer")
    two = groups == 2
    rows, width = rhs.shape[2:]
    modes = basis.shape[-1]
    number = conn_src.shape[-1]
    near, far = near_steps(number), far_steps(columns)
    steps = near + far
    rhs = rhs[0]
    me = lax.axis_index("areal").astype(jnp.int32).reshape(1)
    group = lax.axis_index("layer").astype(jnp.int32).reshape(1)

    tile = pltpu.VMEM((rows, width), BF16)
    pair = pltpu.VMEM((2, rows, width), BF16)
    ask = pltpu.VMEM((8, width), F32)
    part_type = pltpu.VMEM((2, rows, width), F32)
    scratch = [pltpu.VMEM((rows, number * width), BF16), pltpu.VMEM((2, rows, width), F32)]
    one = 2 * rows * width * width

    blocks = held(areal_blocks[0])
    vert = held(vertical_blocks[0])
    rhs_held = held(rhs)

    with jax.named_scope("plan"):
        meta, *asks = call(
            functools.partial(plan_kernel, columns, steps),
            [jax.ShapeDtypeStruct((3 * number,), jnp.int32)] + [ask] * number,
            (conn_src[0, 0], conn_count[0], tile_map, me),
            [SMEM] * 4,
            out_specs=[SMEM] + [VMEM] * number,
        )
        wanted = [shift(x, -k) for x, k in zip(asks, steps)]
        far_sends = call(
            functools.partial(pick_kernel, len(far)),
            [tile] * len(far),
            (rhs_held, *wanted[len(near) :]),
            [VMEM] * (1 + len(far)),
        )

    lam = rhs_held
    sends = [rhs] * len(near) + list(far_sends)
    outer = [rhs]
    pairs = [True] * len(near) + [False] * len(far)
    for step in range(ITERS):
        with jax.named_scope("apply"):
            arrived = [shift(x, k) for x, k in zip(sends, steps)]
            beside = beside_layers(outer, step == 0)
            (part,) = call(
                own_kernel, [part_type], (lam, rhs_held, vert), [VMEM] * 3, flops=2 * one
            )
            part = held(part)
            common = (number, pairs, two, step == 0)
            if step < ITERS - 1:
                lam, *rest = call(
                    functools.partial(apply_kernel, *common),
                    [pair] + [tile] * (number + len(beside)),
                    (meta, group, part, blocks, vert, *arrived, *beside, *wanted),
                    [SMEM] * 2 + [VMEM] * (3 + 2 * number + len(beside)),
                    scratch,
                    flops=2 * number * one,
                )
                lam = held(lam)
                sends, outer = rest[:number], rest[number:]
                pairs = [False] * number
            else:
                adjoint, pieces = call(
                    functools.partial(last_kernel, *common, columns, groups),
                    [
                        jax.ShapeDtypeStruct((2, rows, width), BF16),
                        pltpu.VMEM(
                            (2 * columns, modes // columns // 2, rows) if two else (rows, modes), F32
                        ),
                    ],
                    (meta, group, well_cells[0], well_gain[0], part, blocks, vert, held(sens[0]), held(basis[0]), *arrived, *beside),
                    [SMEM] * 4 + [VMEM] * (5 + number + len(beside)),
                    scratch,
                    flops=2 * number * one,
                )

    with jax.named_scope("project"):
        if two:
            landed = lax.all_to_all(pieces, ("areal", "layer"), 0, 0, tiled=True)
            (coefficients,) = call(
                sum_kernel,
                [jax.ShapeDtypeStruct((rows // 2, modes // columns), BF16)],
                (held(landed),),
                [VMEM],
            )
        else:
            cut = pieces.reshape(groups, rows // groups, columns, modes // columns)
            cut = cut.transpose(2, 0, 1, 3).reshape(columns * groups, rows // groups, modes // columns)
            landed = lax.all_to_all(cut, ("areal", "layer"), 0, 0, tiled=True)
            coefficients = jnp.sum(landed, axis=0).astype(BF16)
    return (adjoint[None], coefficients)


def solution(mesh):
    in_specs = (
        P("areal", "layer", None, None),
        P("areal", "layer", None, None, None),
        P("areal", "layer", None, None, None),
        P("areal", "layer", None),
        P("areal", "layer"),
        P(),
        P("areal", "layer", None),
        P("areal", "layer", None),
        P("areal", "layer", None, None),
        P("areal", "layer", None, None),
    )
    out_specs = (P("areal", "layer", None, None), P("layer", "areal"))
    return jax.shard_map(
        on_device, mesh=mesh, in_specs=in_specs, out_specs=out_specs, check_vma=False
    )
```

time: 314 us -> 94.5 us (0.30)
  waiting for transfers between devices: 245 us -> 20.8 us
  starting transfers between devices: 9.6 us -> 40.9 us
  matrix products: 16.7 us -> 0 us
  between operations: 15.2 us -> 1.49 us
  Pallas kernels: 0 us -> 11.4 us
  local copies, waits for them, and re-layouts: 17.8 us -> 6.55 us
  blocking collectives: 2.59 us -> 13 us
  other arithmetic: 6.32 us -> 0 us
    all_gather x3 -> x0, waiting for transfers between devices: 168 us -> none  [on_device(): whole = lax.all_gather(lam, 'areal', axis=0, tiled=True)]
    reduce_scatter x1 -> x0, waiting for transfers between devices: 73.9 us -> none  [on_device(): lax.psum_scatter(partial_sum, 'areal', scatter_dimension=1, tiled=True)]
    ppermute x6 -> x27, starting transfers between devices: 9.44 us -> 40.9 us  [the longest x24 40.9 us: shift(): lax.ppermute(x, 'areal', [(i, (i - k) % columns) for i in range(columns)])]
    ppermute x6 -> x27, waiting for transfers between devices: 2.97 us -> 20.8 us  [the longest x24 20.8 us: shift(): lax.ppermute(x, 'areal', [(i, (i - k) % columns) for i in range(columns)])]
    dot_general x7 -> x0, matrix products: 16.7 us -> none  [the longest x3 7.65 us: on_device(): jnp.einsum('sru,dsuv->drv', chosen, blocks, preferred_element_type=jnp.fl...]
    all_to_all x0 -> x1, blocking collectives: none -> 13 us  [on_device(): landed = lax.all_to_all(pieces, ('areal', 'layer'), 0, 0, tiled=True)]
    pallas_call x0 -> x9, Pallas kernels: none -> 11.4 us  [call(): pl.pallas_call(kernel, out_shape=outs, in_specs=specs, out_specs=out_spec...]
    gather x4 -> x0, local copies, waits for them, and re-layouts: 10.9 us -> none  [the longest x3 9.65 us: on_device(): chosen = whole[peer, slot]]
  transfers between devices with their start and end apart: 10 -> 27, of which waited for: 6 -> 9; matrix products, arithmetic and copies ran while one was open for 6% -> 0% of each run, Pallas kernels for 0% -> 4%
where the time goes in v1:
time: 94.5 us; the launch traced here: 94.1 us
  starting transfers between devices  40.9 us (43%)
  waiting for transfers between devices  20.8 us (22%)
  blocking collectives  13 us (14%)
  Pallas kernels  11.4 us (12%)
  local copies, waits for them, and re-layouts  6.55 us (7%)
  between operations  1.49 us (2%)
    ppermute x24, starting transfers between devices, shift(): lax.ppermute(x, 'areal', [(i, (i - k) % columns) for i in range(columns)])  40.9 us
    ppermute x24, waiting for transfers between devices, shift(): lax.ppermute(x, 'areal', [(i, (i - k) % columns) for i in range(columns)])  20.8 us
    all_to_all x1, blocking collectives, on_device(): landed = lax.all_to_all(pieces, ('areal', 'layer'), 0, 0, tiled=True)  13 us
    pallas_call x9, Pallas kernels, call(): pl.pallas_call(kernel, out_shape=outs, in_specs=specs, out_specs=out_spec...  11.4 us
    unnamed x24, local copies, waits for them, and re-layouts  6.55 us
  transfers between devices with their start and end apart: 27, of which 9 were waited for; matrix products, arithmetic and copies ran while one was open for 0% of the time, Pallas kernels for 4%

profile of v1, /device:TPU:0, one launch (start us, length us, event | category | flops | bytes accessed | tf_op | source)
XLA Modules:
  0.0 94.1 jit_solution(1295133112866192243)
XLA Ops:
  3.8 4.1 %collective-permute-start.4 = (f32[8,384]{1,0:T(8,128)S(1)}, f32[8,384]{1,0:T(8,128)S(1)}, u32[]{:S(2)}, u32[]{:S(2)}) collective-permute-start(f32[8,384]{1,0:T(8,128)S(1)} %get-tuple-element.30), channel_id=1, source_target_pairs={{0,16},{2,18},{4,20},{6,22},{8,24},{10,26},{12,28},{14,30},{16,0},... | collective-permute-start | bytes 36872 | tf_op jit(solution)/shard_map/plan/ppermute | solution.py:173
  7.9 1.3 %collective-permute-start.5 = (f32[8,384]{1,0:T(8,128)S(1)}, f32[8,384]{1,0:T(8,128)S(1)}, u32[]{:S(2)}, u32[]{:S(2)}) collective-permute-start(f32[8,384]{1,0:T(8,128)S(1)} %get-tuple-element.31), channel_id=1, source_target_pairs={{0,18},{2,20},{4,22},{6,24},{8,26},{10,28},{12,30},{14,0},{16,2},{... | collective-permute-start | bytes 36872 | tf_op jit(solution)/shard_map/plan/ppermute | solution.py:173
  9.6 3.8 %collective-permute-done.5.refs_1_.refs_12_ = f32[8,384]{1,0:T(8,128)S(1)} collective-permute-done((f32[8,384]{1,0:T(8,128)S(1)}, f32[8,384]{1,0:T(8,128)S(1)}, u32[]{:S(2)}, u32[]{:S(2)}) %collective-permute-start.5) | collective-permute-done | bytes 12320 | tf_op jit(solution)/shard_map/plan/ppermute | solution.py:173
  14.5 3.7 %collective-permute-start.7 = (bf16[112,384]{1,0:T(8,128)(2,1)S(1)}, bf16[112,384]{1,0:T(8,128)(2,1)S(1)}, u32[]{:S(2)}, u32[]{:S(2)}) collective-permute-start(bf16[112,384]{1,0:T(8,128)(2,1)S(1)} %get-tuple-element.33), channel_id=1, source_target_pairs={{0,14},{2,16},{4,18},{6,20},{8,22},{10,24},{12,26},{14,28},{16,30}... | collective-permute-start | bytes 258056 | tf_op jit(solution)/shard_map/apply/ppermute | solution.py:173
  18.2 1.5 %collective-permute-start.10 = (f32[8,384]{1,0:T(8,128)S(1)}, f32[8,384]{1,0:T(8,128)S(1)}, u32[]{:S(2)}, u32[]{:S(2)}) collective-permute-start(f32[8,384]{1,0:T(8,128)S(1)} %get-tuple-element.35), channel_id=1, source_target_pairs={{0,4},{2,6},{4,8},{6,10},{8,12},{10,14},{12,16},{14,18},{16,20},{1... | collective-permute-start | bytes 36872 | tf_op jit(solution)/shard_map/plan/ppermute | solution.py:173
  19.7 3.2 %collective-permute-start.11 = (f32[8,384]{1,0:T(8,128)S(1)}, f32[8,384]{1,0:T(8,128)S(1)}, u32[]{:S(2)}, u32[]{:S(2)}) collective-permute-start(f32[8,384]{1,0:T(8,128)S(1)} %get-tuple-element.36), channel_id=1, source_target_pairs={{0,30},{2,0},{4,2},{6,4},{8,6},{10,8},{12,10},{14,12},{16,14},{18,... | collective-permute-start | bytes 36872 | tf_op jit(solution)/shard_map/plan/ppermute | solution.py:173
  25.3 5.0 %collective-permute-start = (bf16[2,112,384]{2,1,0:T(8,128)(2,1)}, bf16[2,112,384]{2,1,0:T(8,128)(2,1)S(1)}, u32[]{:S(2)}, u32[]{:S(2)}) collective-permute-start(bf16[2,112,384]{2,1,0:T(8,128)(2,1)} %bitcast.6.lam.rhs), channel_id=1, source_target_pairs={{0,30},{2,0},{4,2},{6,4},{8,6},{10,8},{12,10},{14,12},{16,14},{18,... | collective-permute-start | bytes 516104 | tf_op jit(solution)/shard_map/apply/ppermute | solution.py:173
  30.4 1.7 %collective-permute-done.9.refs_7_ = f32[8,384]{1,0:T(8,128)S(1)} collective-permute-done((f32[8,384]{1,0:T(8,128)S(1)}, f32[8,384]{1,0:T(8,128)S(1)}, u32[]{:S(2)}, u32[]{:S(2)}) %collective-permute-start.9) | collective-permute-done | bytes 12320 | tf_op jit(solution)/shard_map/plan/ppermute | solution.py:173
  32.5 1.3 %copy-done = bf16[1,2,2,384,384]{4,3,2,1,0:T(8,128)(2,1)S(1)} copy-done((bf16[1,2,2,384,384]{4,3,2,1,0:T(8,128)(2,1)S(1)}, bf16[1,2,2,384,384]{4,3,2,1,0:T(8,128)(2,1)}, u32[]{:S(2)}) %copy-start) | copy-done | bytes 1179672
  33.7 1.4 %apply.6.part = f32[2,112,384]{2,1,0:T(8,128)S(1)} custom-call(bf16[2,112,384]{2,1,0:T(8,128)(2,1)} %bitcast.6.lam.rhs, bf16[2,112,384]{2,1,0:T(8,128)(2,1)} %bitcast.6.lam.rhs, bf16[2,2,384,384]{3,2,1,0:T(8,128)(2,1)S(1)} %bitcast.15), custom_call_target="tpu_custom_call" | custom-call | flops 66060288 | bytes 330301 | tf_op jit(solution)/shard_map/apply/pallas_call | solution.py:160
  35.1 7.4 %collective-permute-done.1.refs_1_ = bf16[2,112,384]{2,1,0:T(8,128)(2,1)S(1)} collective-permute-done((bf16[2,112,384]{2,1,0:T(8,128)(2,1)}, bf16[2,112,384]{2,1,0:T(8,128)(2,1)S(1)}, u32[]{:S(2)}, u32[]{:S(2)}) %collective-permute-start.1) | collective-permute-done | bytes 172064 | tf_op jit(solution)/shard_map/apply/ppermute | solution.py:173
  43.8 2.0 %copy-done.3 = bf16[1,2,6,384,384]{4,3,2,1,0:T(8,128)(2,1)S(1)} copy-done((bf16[1,2,6,384,384]{4,3,2,1,0:T(8,128)(2,1)S(1)}, bf16[1,2,6,384,384]{4,3,2,1,0:T(8,128)(2,1)}, u32[]{:S(2)}) %copy-start.3) | copy-done | bytes 3538968
  45.8 1.6 %apply.7 = (bf16[2,112,384]{2,1,0:T(8,128)(2,1)S(1)}, bf16[112,384]{1,0:T(8,128)(2,1)S(1)}, bf16[112,384]{1,0:T(8,128)(2,1)S(1)}, bf16[112,384]{1,0:T(8,128)(2,1...) custom-call(s32[18]{0:T(128)S(1)} %get-tuple-element.29.meta, ...), custom_call_target="tpu_custom_call" | custom-call | flops 396361728 | bytes 1981808 | tf_op jit(solution)/shard_map/apply/pallas_call | solution.py:160
  49.5 2.0 %collective-permute-start.16 = (bf16[112,384]{1,0:T(8,128)(2,1)S(1)}, bf16[112,384]{1,0:T(8,128)(2,1)S(1)}, u32[]{:S(2)}, u32[]{:S(2)}) collective-permute-start(bf16[112,384]{1,0:T(8,128)(2,1)S(1)} %get-tuple-element.42), channel_id=1, source_target_pairs={{0,4},{2,6},{4,8},{6,10},{8,12},{10,14},{12,16},{14,18},{16,20},{1... | collective-permute-start | bytes 258056 | tf_op jit(solution)/shard_map/apply/ppermute | solution.py:173
  52.7 4.2 %collective-permute-start.18 = (bf16[112,384]{1,0:T(8,128)(2,1)S(1)}, bf16[112,384]{1,0:T(8,128)(2,1)S(1)}, u32[]{:S(2)}, u32[]{:S(2)}) collective-permute-start(bf16[112,384]{1,0:T(8,128)(2,1)S(1)} %get-tuple-element.44), channel_id=1, source_target_pairs={{0,14},{2,16},{4,18},{6,20},{8,22},{10,24},{12,26},{14,28},{16,30}... | collective-permute-start | bytes 258056 | tf_op jit(solution)/shard_map/apply/ppermute | solution.py:173
  58.2 2.1 %collective-permute-done.18.refs_5_ = bf16[112,384]{1,0:T(8,128)(2,1)S(1)} collective-permute-done((bf16[112,384]{1,0:T(8,128)(2,1)S(1)}, bf16[112,384]{1,0:T(8,128)(2,1)S(1)}, u32[]{:S(2)}, u32[]{:S(2)}) %collective-permute-start.18) | collective-permute-done | bytes 86048 | tf_op jit(solution)/shard_map/apply/ppermute | solution.py:173
  60.3 1.6 %apply.9 = (bf16[2,112,384]{2,1,0:T(8,128)(2,1)S(1)}, bf16[112,384]{1,0:T(8,128)(2,1)S(1)}, bf16[112,384]{1,0:T(8,128)(2,1)S(1)}, bf16[112,384]{1,0:T(8,128)(2,1...) custom-call(s32[18]{0:T(128)S(1)} %get-tuple-element.29.meta, ...), custom_call_target="tpu_custom_call" | custom-call | flops 396361728 | bytes 1981808 | tf_op jit(solution)/shard_map/apply/pallas_call | solution.py:160
  61.9 3.7 %collective-permute-start.20 = (bf16[112,384]{1,0:T(8,128)(2,1)S(1)}, bf16[112,384]{1,0:T(8,128)(2,1)S(1)}, u32[]{:S(2)}, u32[]{:S(2)}) collective-permute-start(bf16[112,384]{1,0:T(8,128)(2,1)S(1)} %get-tuple-element.47), channel_id=1, source_target_pairs={{0,30},{2,0},{4,2},{6,4},{8,6},{10,8},{12,10},{14,12},{16,14},{18,... | collective-permute-start | bytes 258056 | tf_op jit(solution)/shard_map/apply/ppermute | solution.py:173
  66.5 2.0 %collective-permute-start.22 = (bf16[112,384]{1,0:T(8,128)(2,1)S(1)}, bf16[112,384]{1,0:T(8,128)(2,1)S(1)}, u32[]{:S(2)}, u32[]{:S(2)}) collective-permute-start(bf16[112,384]{1,0:T(8,128)(2,1)S(1)} %get-tuple-element.49), channel_id=1, source_target_pairs={{0,2},{2,4},{4,6},{6,8},{8,10},{10,12},{12,14},{14,16},{16,18},{18... | collective-permute-start | bytes 258056 | tf_op jit(solution)/shard_map/apply/ppermute | solution.py:173
  68.5 5.3 %collective-permute-start.25 = (bf16[112,384]{1,0:T(8,128)(2,1)S(1)}, bf16[112,384]{1,0:T(8,128)(2,1)S(1)}, u32[]{:S(2)}, u32[]{:S(2)}) collective-permute-start(bf16[112,384]{1,0:T(8,128)(2,1)S(1)} %get-tuple-element.52), channel_id=1, source_target_pairs={{0,14},{2,16},{4,18},{6,20},{8,22},{10,24},{12,26},{14,28},{16,30}... | collective-permute-start | bytes 258056 | tf_op jit(solution)/shard_map/apply/ppermute | solution.py:173
  75.0 1.4 %collective-permute-done.23.refs_3_ = bf16[112,384]{1,0:T(8,128)(2,1)S(1)} collective-permute-done((bf16[112,384]{1,0:T(8,128)(2,1)S(1)}, bf16[112,384]{1,0:T(8,128)(2,1)S(1)}, u32[]{:S(2)}, u32[]{:S(2)}) %collective-permute-start.23) | collective-permute-done | bytes 86048 | tf_op jit(solution)/shard_map/apply/ppermute | solution.py:173
  76.4 1.7 %collective-permute-done.25.refs_5_ = bf16[112,384]{1,0:T(8,128)(2,1)S(1)} collective-permute-done((bf16[112,384]{1,0:T(8,128)(2,1)S(1)}, bf16[112,384]{1,0:T(8,128)(2,1)S(1)}, u32[]{:S(2)}, u32[]{:S(2)}) %collective-permute-start.25) | collective-permute-done | bytes 86048 | tf_op jit(solution)/shard_map/apply/ppermute | solution.py:173
  78.1 2.2 %apply.11 = (bf16[2,112,384]{2,1,0:T(8,128)(2,1)}, f32[32,8,112]{2,1,0:T(8,128)S(1)}) custom-call(s32[18]{0:T(128)S(1)} %get-tuple-element.29.meta, s32[1]{0:T(128)} %bitcast.3.group, s32[2,4]{1,0:T(2,128)S(1)} %bitcast.26, f32[2,4]{1,0:T(2,128)S(1)} %bitcast.27, f32[2,112,384]{2,1,0:T(8,128)S(1)} %apply.10.part, bf16[2,6,384,384]{3,2,1,0:T(8,128)(2,1)S(1)} %bitcast.23, ...), custom_call_target="tpu_custom_call" | custom-call | flops 396361728 | bytes 1981808 | tf_op jit(solution)/shard_map/apply/pallas_call | solution.py:160
  80.3 13.0 %all_to_all.5.pieces = f32[32,8,112]{2,1,0:T(8,128)S(1)} all-to-all(f32[32,8,112]{2,1,0:T(8,128)S(1)} %get-tuple-element.55), channel_id=1, replica_groups=mesh['areal'=16,'layer'=2] {'areal','layer'}, dimensions={0} | all-to-all | bytes 229376 | tf_op jit(solution)/shard_map/project/all_to_all | solution.py:279
  (64 shorter events, 15.7 us)
Async XLA Ops:
  3.8 5.8 %collective-permute-start.4 = (f32[8,384]{1,0:T(8,128)S(1)}, f32[8,384]{1,0:T(8,128)S(1)}, u32[]{:S(2)}, u32[]{:S(2)}) collective-permute-start(f32[8,384]{1,0:T(8,128)S(1)} %get-tuple-element.30), channel_id=1, source_target_pairs={{0,16},{2,18},{4,20},{6,22},{8,24},{10,26},{12,28},{14,30},{16,0},... | collective-permute-start | bytes 36872 | tf_op jit(solution)/shard_map/plan/ppermute | solution.py:173
  7.9 5.5 %collective-permute-start.5 = (f32[8,384]{1,0:T(8,128)S(1)}, f32[8,384]{1,0:T(8,128)S(1)}, u32[]{:S(2)}, u32[]{:S(2)}) collective-permute-start(f32[8,384]{1,0:T(8,128)S(1)} %get-tuple-element.31), channel_id=1, source_target_pairs={{0,18},{2,20},{4,22},{6,24},{8,26},{10,28},{12,30},{14,0},{16,2},{... | collective-permute-start | bytes 36872 | tf_op jit(solution)/shard_map/plan/ppermute | solution.py:173
  14.4 17.7 %collective-permute-start.6 = (bf16[112,384]{1,0:T(8,128)(2,1)S(1)}, bf16[112,384]{1,0:T(8,128)(2,1)S(1)}, u32[]{:S(2)}, u32[]{:S(2)}) collective-permute-start(bf16[112,384]{1,0:T(8,128)(2,1)S(1)} %get-tuple-element.32), channel_id=1, source_target_pairs={{0,16},{2,18},{4,20},{6,22},{8,24},{10,26},{12,28},{14,30},{16,0},... | collective-permute-start | bytes 258056 | tf_op jit(solution)/shard_map/apply/ppermute | solution.py:173
  14.5 17.9 %collective-permute-start.7 = (bf16[112,384]{1,0:T(8,128)(2,1)S(1)}, bf16[112,384]{1,0:T(8,128)(2,1)S(1)}, u32[]{:S(2)}, u32[]{:S(2)}) collective-permute-start(bf16[112,384]{1,0:T(8,128)(2,1)S(1)} %get-tuple-element.33), channel_id=1, source_target_pairs={{0,14},{2,16},{4,18},{6,20},{8,22},{10,24},{12,26},{14,28},{16,30}... | collective-permute-start | bytes 258056 | tf_op jit(solution)/shard_map/apply/ppermute | solution.py:173
  18.2 6.5 %collective-permute-start.10 = (f32[8,384]{1,0:T(8,128)S(1)}, f32[8,384]{1,0:T(8,128)S(1)}, u32[]{:S(2)}, u32[]{:S(2)}) collective-permute-start(f32[8,384]{1,0:T(8,128)S(1)} %get-tuple-element.35), channel_id=1, source_target_pairs={{0,4},{2,6},{4,8},{6,10},{8,12},{10,14},{12,16},{14,18},{16,20},{1... | collective-permute-start | bytes 36872 | tf_op jit(solution)/shard_map/plan/ppermute | solution.py:173
  19.7 5.6 %collective-permute-start.11 = (f32[8,384]{1,0:T(8,128)S(1)}, f32[8,384]{1,0:T(8,128)S(1)}, u32[]{:S(2)}, u32[]{:S(2)}) collective-permute-start(f32[8,384]{1,0:T(8,128)S(1)} %get-tuple-element.36), channel_id=1, source_target_pairs={{0,30},{2,0},{4,2},{6,4},{8,6},{10,8},{12,10},{14,12},{16,14},{18,... | collective-permute-start | bytes 36872 | tf_op jit(solution)/shard_map/plan/ppermute | solution.py:173
  23.0 7.4 %collective-permute-start.12 = (f32[8,384]{1,0:T(8,128)S(1)}, f32[8,384]{1,0:T(8,128)S(1)}, u32[]{:S(2)}, u32[]{:S(2)}) collective-permute-start(f32[8,384]{1,0:T(8,128)S(1)} %get-tuple-element.37), channel_id=1, source_target_pairs={{0,28},{2,30},{4,0},{6,2},{8,4},{10,6},{12,8},{14,10},{16,12},{18,... | collective-permute-start | bytes 36872 | tf_op jit(solution)/shard_map/plan/ppermute | solution.py:173
  24.7 7.3 %collective-permute-start.9 = (f32[8,384]{1,0:T(8,128)S(1)}, f32[8,384]{1,0:T(8,128)S(1)}, u32[]{:S(2)}, u32[]{:S(2)}) collective-permute-start(f32[8,384]{1,0:T(8,128)S(1)} %get-tuple-element.34), channel_id=1, source_target_pairs={{0,2},{2,4},{4,6},{6,8},{8,10},{10,12},{12,14},{14,16},{16,18},{18... | collective-permute-start | bytes 36872 | tf_op jit(solution)/shard_map/plan/ppermute | solution.py:173
  25.3 9.8 %collective-permute-start = (bf16[2,112,384]{2,1,0:T(8,128)(2,1)}, bf16[2,112,384]{2,1,0:T(8,128)(2,1)S(1)}, u32[]{:S(2)}, u32[]{:S(2)}) collective-permute-start(bf16[2,112,384]{2,1,0:T(8,128)(2,1)} %bitcast.6.lam.rhs), channel_id=1, source_target_pairs={{0,30},{2,0},{4,2},{6,4},{8,6},{10,8},{12,10},{14,12},{16,14},{18,... | collective-permute-start | bytes 516104 | tf_op jit(solution)/shard_map/apply/ppermute | solution.py:173
  30.4 12.2 %collective-permute-start.1 = (bf16[2,112,384]{2,1,0:T(8,128)(2,1)}, bf16[2,112,384]{2,1,0:T(8,128)(2,1)S(1)}, u32[]{:S(2)}, u32[]{:S(2)}) collective-permute-start(bf16[2,112,384]{2,1,0:T(8,128)(2,1)} %bitcast.6.lam.rhs), channel_id=1, source_target_pairs={{0,28},{2,30},{4,0},{6,2},{8,4},{10,6},{12,8},{14,10},{16,12},{18,... | collective-permute-start | bytes 516104 | tf_op jit(solution)/shard_map/apply/ppermute | solution.py:173
  32.0 10.5 %collective-permute-start.2 = (bf16[2,112,384]{2,1,0:T(8,128)(2,1)}, bf16[2,112,384]{2,1,0:T(8,128)(2,1)S(1)}, u32[]{:S(2)}, u32[]{:S(2)}) collective-permute-start(bf16[2,112,384]{2,1,0:T(8,128)(2,1)} %bitcast.6.lam.rhs), channel_id=1, source_target_pairs={{0,2},{2,4},{4,6},{6,8},{8,10},{10,12},{12,14},{14,16},{16,18},{18... | collective-permute-start | bytes 516104 | tf_op jit(solution)/shard_map/apply/ppermute | solution.py:173
  32.0 10.5 %collective-permute-start.3 = (bf16[2,112,384]{2,1,0:T(8,128)(2,1)}, bf16[2,112,384]{2,1,0:T(8,128)(2,1)S(1)}, u32[]{:S(2)}, u32[]{:S(2)}) collective-permute-start(bf16[2,112,384]{2,1,0:T(8,128)(2,1)} %bitcast.6.lam.rhs), channel_id=1, source_target_pairs={{0,4},{2,6},{4,8},{6,10},{8,12},{10,14},{12,16},{14,18},{16,20},{1... | collective-permute-start | bytes 516104 | tf_op jit(solution)/shard_map/apply/ppermute | solution.py:173
  32.5 10.1 %collective-permute-start.8 = (bf16[2,112,384]{2,1,0:T(8,128)(2,1)}, bf16[2,112,384]{2,1,0:T(8,128)(2,1)S(1)}, u32[]{:S(2)}, u32[]{:S(2)}) collective-permute-start(bf16[2,112,384]{2,1,0:T(8,128)(2,1)} %bitcast.6.lam.rhs), channel_id=1, source_target_pairs={{0,1},{1,0},{2,3},{3,2},{4,5},{5,4},{6,7},{7,6},{8,9},{9,8},{10,11... | collective-permute-start | bytes 516104 | tf_op jit(solution)/shard_map/apply/ppermute | solution.py:179
  48.7 8.2 %collective-permute-start.14 = (bf16[112,384]{1,0:T(8,128)(2,1)S(1)}, bf16[112,384]{1,0:T(8,128)(2,1)S(1)}, u32[]{:S(2)}, u32[]{:S(2)}) collective-permute-start(bf16[112,384]{1,0:T(8,128)(2,1)S(1)} %get-tuple-element.40), channel_id=1, source_target_pairs={{0,28},{2,30},{4,0},{6,2},{8,4},{10,6},{12,8},{14,10},{16,12},{18,... | collective-permute-start | bytes 258056 | tf_op jit(solution)/shard_map/apply/ppermute | solution.py:173
  48.7 9.5 %collective-permute-start.15 = (bf16[112,384]{1,0:T(8,128)(2,1)S(1)}, bf16[112,384]{1,0:T(8,128)(2,1)S(1)}, u32[]{:S(2)}, u32[]{:S(2)}) collective-permute-start(bf16[112,384]{1,0:T(8,128)(2,1)S(1)} %get-tuple-element.41), channel_id=1, source_target_pairs={{0,2},{2,4},{4,6},{6,8},{8,10},{10,12},{12,14},{14,16},{16,18},{18... | collective-permute-start | bytes 258056 | tf_op jit(solution)/shard_map/apply/ppermute | solution.py:173
  49.5 8.7 %collective-permute-start.16 = (bf16[112,384]{1,0:T(8,128)(2,1)S(1)}, bf16[112,384]{1,0:T(8,128)(2,1)S(1)}, u32[]{:S(2)}, u32[]{:S(2)}) collective-permute-start(bf16[112,384]{1,0:T(8,128)(2,1)S(1)} %get-tuple-element.42), channel_id=1, source_target_pairs={{0,4},{2,6},{4,8},{6,10},{8,12},{10,14},{12,16},{14,18},{16,20},{1... | collective-permute-start | bytes 258056 | tf_op jit(solution)/shard_map/apply/ppermute | solution.py:173
  51.5 6.7 %collective-permute-start.17 = (bf16[112,384]{1,0:T(8,128)(2,1)S(1)}, bf16[112,384]{1,0:T(8,128)(2,1)S(1)}, u32[]{:S(2)}, u32[]{:S(2)}) collective-permute-start(bf16[112,384]{1,0:T(8,128)(2,1)S(1)} %get-tuple-element.43), channel_id=1, source_target_pairs={{0,16},{2,18},{4,20},{6,22},{8,24},{10,26},{12,28},{14,30},{16,0},... | collective-permute-start | bytes 258056 | tf_op jit(solution)/shard_map/apply/ppermute | solution.py:173
  52.7 7.6 %collective-permute-start.18 = (bf16[112,384]{1,0:T(8,128)(2,1)S(1)}, bf16[112,384]{1,0:T(8,128)(2,1)S(1)}, u32[]{:S(2)}, u32[]{:S(2)}) collective-permute-start(bf16[112,384]{1,0:T(8,128)(2,1)S(1)} %get-tuple-element.44), channel_id=1, source_target_pairs={{0,14},{2,16},{4,18},{6,20},{8,22},{10,24},{12,26},{14,28},{16,30}... | collective-permute-start | bytes 258056 | tf_op jit(solution)/shard_map/apply/ppermute | solution.py:173
  61.9 6.6 %collective-permute-start.20 = (bf16[112,384]{1,0:T(8,128)(2,1)S(1)}, bf16[112,384]{1,0:T(8,128)(2,1)S(1)}, u32[]{:S(2)}, u32[]{:S(2)}) collective-permute-start(bf16[112,384]{1,0:T(8,128)(2,1)S(1)} %get-tuple-element.47), channel_id=1, source_target_pairs={{0,30},{2,0},{4,2},{6,4},{8,6},{10,8},{12,10},{14,12},{16,14},{18,... | collective-permute-start | bytes 258056 | tf_op jit(solution)/shard_map/apply/ppermute | solution.py:173
  65.6 8.2 %collective-permute-start.21 = (bf16[112,384]{1,0:T(8,128)(2,1)S(1)}, bf16[112,384]{1,0:T(8,128)(2,1)S(1)}, u32[]{:S(2)}, u32[]{:S(2)}) collective-permute-start(bf16[112,384]{1,0:T(8,128)(2,1)S(1)} %get-tuple-element.48), channel_id=1, source_target_pairs={{0,28},{2,30},{4,0},{6,2},{8,4},{10,6},{12,8},{14,10},{16,12},{18,... | collective-permute-start | bytes 258056 | tf_op jit(solution)/shard_map/apply/ppermute | solution.py:173
  66.5 8.5 %collective-permute-start.22 = (bf16[112,384]{1,0:T(8,128)(2,1)S(1)}, bf16[112,384]{1,0:T(8,128)(2,1)S(1)}, u32[]{:S(2)}, u32[]{:S(2)}) collective-permute-start(bf16[112,384]{1,0:T(8,128)(2,1)S(1)} %get-tuple-element.49), channel_id=1, source_target_pairs={{0,2},{2,4},{4,6},{6,8},{8,10},{10,12},{12,14},{14,16},{16,18},{18... | collective-permute-start | bytes 258056 | tf_op jit(solution)/shard_map/apply/ppermute | solution.py:173
  68.5 7.9 %collective-permute-start.23 = (bf16[112,384]{1,0:T(8,128)(2,1)S(1)}, bf16[112,384]{1,0:T(8,128)(2,1)S(1)}, u32[]{:S(2)}, u32[]{:S(2)}) collective-permute-start(bf16[112,384]{1,0:T(8,128)(2,1)S(1)} %get-tuple-element.50), channel_id=1, source_target_pairs={{0,4},{2,6},{4,8},{6,10},{8,12},{10,14},{12,16},{14,18},{16,20},{1... | collective-permute-start | bytes 258056 | tf_op jit(solution)/shard_map/apply/ppermute | solution.py:173
  68.5 7.9 %collective-permute-start.24 = (bf16[112,384]{1,0:T(8,128)(2,1)S(1)}, bf16[112,384]{1,0:T(8,128)(2,1)S(1)}, u32[]{:S(2)}, u32[]{:S(2)}) collective-permute-start(bf16[112,384]{1,0:T(8,128)(2,1)S(1)} %get-tuple-element.51), channel_id=1, source_target_pairs={{0,16},{2,18},{4,20},{6,22},{8,24},{10,26},{12,28},{14,30},{16,0},... | collective-permute-start | bytes 258056 | tf_op jit(solution)/shard_map/apply/ppermute | solution.py:173
  68.5 9.6 %collective-permute-start.25 = (bf16[112,384]{1,0:T(8,128)(2,1)S(1)}, bf16[112,384]{1,0:T(8,128)(2,1)S(1)}, u32[]{:S(2)}, u32[]{:S(2)}) collective-permute-start(bf16[112,384]{1,0:T(8,128)(2,1)S(1)} %get-tuple-element.52), channel_id=1, source_target_pairs={{0,14},{2,16},{4,18},{6,20},{8,22},{10,24},{12,26},{14,28},{16,30}... | collective-permute-start | bytes 258056 | tf_op jit(solution)/shard_map/apply/ppermute | solution.py:173
  (14 other events, 133.5 us)
